TPU v7x, 128 devices: a whole 4x4x4 slice. The times are simulated.
128 devices in a mesh: rows: 4 (over x), prefix: 32 (over z, y, core).
Axes of the slice: x: 4, y: 4, z: 4, core: 2. Of those that a mesh axis runs over, the one named last changes fastest.
Arguments:
- queries: bfloat16 [4, 128, 32, 128], P(None, ('rows', 'prefix')), may hold values from -16 to 16
- new_kv: bfloat16 [2, 4, 128, 16, 128], P(None, None, ('rows', 'prefix')), may hold values from -16 to 16
- suffix_kv: bfloat16 [2, 128, 256, 16, 128], P(None, ('rows', 'prefix')), may hold values from -16 to 16
- suffix_len: int32 [128], P(('rows', 'prefix')), may hold values from 1 to 256, as said below
- prefix_len: int32 [8], replicated, may hold values from 19457 to 40960, as said below
- prefix_kv: bfloat16 [2, 320, 16, 1024, 128], P(None, 'prefix', 'rows'), may hold values from -16 to 16
- block_prompt: int32 [32, 10], P('prefix'), may hold values from 0 to 7, as said below
- block_index: int32 [32, 10], P('prefix'), may hold values from 0 to 39, as said below
- block_count: int32 [32], P('prefix'), may hold values from 1 to 10, as said below
Outputs:
- attention: bfloat16 [4, 128, 4096], P(None, ('rows', 'prefix'))
Inputs may be any that keep to these rules, and one draw needn't show every extreme that they name: `block_count`: some owner uses all 10 slots in every draw. `block_prompt`: 0 in unused slots; every block of every prompt lies in exactly one used slot; an owner's used slots hold only blocks of the prompt of its first used slot and of the prompt of its last used slot. `block_index`: 0 in unused slots; a prompt's blocks are numbered from 0; some prompt has 16 * 10 // 4 blocks in every draw. Prompt p has exactly ceil(prefix_len[p] / 1024) blocks; the longest prompt reaches the maximum in every draw. `suffix_len`: some row has 256 in every draw.
All inputs are finite; a program needn't handle non-finite values.
Results may differ from a plain program's by a relative error of at most 0.004.
Values may be sent and summed in bfloat16 or wider, within the bound.
A program may use at most 128 MiB of HBM per device.

v0:
```python
import jax
import jax.numpy as jnp
from jax import lax
from jax.sharding import PartitionSpec as P

SAMPLES = 16


masked_score = -1e30
score_scale = 168.0 ** (-0.5)


def local(
    queries,
    new_kv,
    suffix_kv,
    suffix_len,
    prefix_len,
    prefix_kv,
    block_prompt,
    block_index,
    block_count,
):
    steps, rows_dev, heads, width = queries.shape
    kv_heads = suffix_kv.shape[3]
    kv_local = prefix_kv.shape[2]
    block_len = prefix_kv.shape[3]
    suffix_slots = suffix_kv.shape[2]
    n_rows = lax.axis_size("rows")
    n_prefix = lax.axis_size("prefix")
    heads_local = heads // n_rows
    group = heads // kv_heads
    total_rows = rows_dev * n_rows * n_prefix
    gathered = lax.all_gather(queries, "prefix", axis=1, tiled=True)
    local_q = lax.all_to_all(gathered, "rows", split_axis=2, concat_axis=1, tiled=True)
    positions = jnp.arange(block_len, dtype=jnp.int32)

    def visit(slot_number, carry):
        peak_rows, mass_rows, sum_rows = carry
        prompt = block_prompt[0, slot_number]
        block_number = block_index[0, slot_number]
        first_row = prompt * SAMPLES
        chosen = lax.dynamic_slice_in_dim(local_q, first_row, SAMPLES, 1)
        chosen = chosen.reshape(steps, SAMPLES, kv_local, group, width).transpose(2, 3, 0, 1, 4)
        chosen = chosen.reshape(kv_local, group * steps * SAMPLES, width)
        key_block = prefix_kv[0, slot_number]
        value_block = prefix_kv[1, slot_number]
        scores = (
            jnp.einsum("kqd,kbd->kqb", chosen, key_block, preferred_element_type=jnp.float32)
            * score_scale
        )
        live = block_number * block_len + positions < prefix_len[prompt]
        scores = jnp.where(live, scores, masked_score)
        block_peak = jnp.max(scores, axis=-1)
        weights = jnp.where(live, jnp.exp(scores - block_peak[..., None]), 0.0).astype(jnp.bfloat16)
        block_mass = jnp.sum(weights, axis=-1, dtype=jnp.float32)
        block_sum = jnp.einsum(
            "kqb,kbd->kqd", weights, value_block, preferred_element_type=jnp.float32
        )
        block_peak = (
            block_peak.reshape(kv_local, group, steps, SAMPLES)
            .transpose(3, 2, 0, 1)
            .reshape(SAMPLES, steps, heads_local)
        )
        block_mass = (
            block_mass.reshape(kv_local, group, steps, SAMPLES)
            .transpose(3, 2, 0, 1)
            .reshape(SAMPLES, steps, heads_local)
        )
        block_sum = block_sum.reshape(kv_local, group, steps, SAMPLES, width).transpose(
            3, 2, 0, 1, 4
        )
        block_sum = block_sum.reshape(SAMPLES, steps, heads_local, width)
        old_peak = lax.dynamic_slice_in_dim(peak_rows, first_row, SAMPLES, 0)
        old_mass = lax.dynamic_slice_in_dim(mass_rows, first_row, SAMPLES, 0)
        old_sum = lax.dynamic_slice_in_dim(sum_rows, first_row, SAMPLES, 0)
        new_peak = jnp.maximum(old_peak, block_peak)
        keep_old = jnp.exp(old_peak - new_peak)
        take_new = jnp.exp(block_peak - new_peak)
        peak_rows = lax.dynamic_update_slice_in_dim(peak_rows, new_peak, first_row, 0)
        mass_rows = lax.dynamic_update_slice_in_dim(
            mass_rows, keep_old * old_mass + take_new * block_mass, first_row, 0
        )
        sum_rows = lax.dynamic_update_slice_in_dim(
            sum_rows, keep_old[..., None] * old_sum + take_new[..., None] * block_sum, first_row, 0
        )
        return (peak_rows, mass_rows, sum_rows)

    peak_init = jnp.full((total_rows, steps, heads_local), masked_score, jnp.float32)
    mass_init = jnp.zeros((total_rows, steps, heads_local), jnp.float32)
    sum_init = jnp.zeros((total_rows, steps, heads_local, width), jnp.float32)
    peak_rows, mass_rows, sum_rows = lax.fori_loop(
        0, block_count[0], visit, (peak_init, mass_init, sum_init)
    )
    shared_peak = lax.pmax(peak_rows, "prefix")
    factor = jnp.exp(peak_rows - shared_peak)
    mass_rows = mass_rows * factor
    sum_rows = sum_rows * factor[..., None]
    mass_rows, sum_rows, shared_peak = (
        lax.all_to_all(mass_rows, "rows", split_axis=0, concat_axis=2, tiled=True),
        lax.all_to_all(sum_rows, "rows", split_axis=0, concat_axis=2, tiled=True),
        lax.all_to_all(shared_peak, "rows", split_axis=0, concat_axis=2, tiled=True),
    )
    mass_rows, sum_rows = (
        lax.psum_scatter(mass_rows, "prefix", scatter_dimension=0, tiled=True),
        lax.psum_scatter(sum_rows, "prefix", scatter_dimension=0, tiled=True),
    )
    shared_peak = lax.dynamic_slice_in_dim(
        shared_peak, lax.axis_index("prefix") * rows_dev, rows_dev, 0
    )
    prefix_peak = shared_peak.transpose(1, 0, 2)
    prefix_mass = mass_rows.transpose(1, 0, 2)
    prefix_sum = sum_rows.transpose(1, 0, 2, 3)
    query_rows = queries.reshape(steps, rows_dev, kv_heads, group, width)
    far = (
        jnp.einsum(
            "trkgd,rpkd->trkgp", query_rows, suffix_kv[0], preferred_element_type=jnp.float32
        )
        * score_scale
    )
    near = (
        jnp.einsum("trkgd,prkd->trkgp", query_rows, new_kv[0], preferred_element_type=jnp.float32)
        * score_scale
    )
    far_live = (jnp.arange(suffix_slots, dtype=jnp.int32)[None, :] < suffix_len[:, None])[
        None, :, None, None, :
    ]
    step_ids = jnp.arange(steps, dtype=jnp.int32)
    near_live = (step_ids[None, :] <= step_ids[:, None])[:, None, None, None, :]
    far = jnp.where(far_live, far, masked_score)
    near = jnp.where(near_live, near, masked_score)
    own_peak = jnp.maximum(jnp.max(far, axis=-1), jnp.max(near, axis=-1))
    far_weights = jnp.where(far_live, jnp.exp(far - own_peak[..., None]), 0.0).astype(jnp.bfloat16)
    near_weights = jnp.where(near_live, jnp.exp(near - own_peak[..., None]), 0.0).astype(
        jnp.bfloat16
    )
    own_mass = jnp.sum(far_weights, axis=-1, dtype=jnp.float32) + jnp.sum(
        near_weights, axis=-1, dtype=jnp.float32
    )
    own_sum = jnp.einsum(
        "trkgp,rpkd->trkgd", far_weights, suffix_kv[1], preferred_element_type=jnp.float32
    )
    own_sum = own_sum + jnp.einsum(
        "trkgp,prkd->trkgd", near_weights, new_kv[1], preferred_element_type=jnp.float32
    )
    own_peak = own_peak.reshape(steps, rows_dev, heads)
    own_mass = own_mass.reshape(steps, rows_dev, heads)
    own_sum = own_sum.reshape(steps, rows_dev, heads, width)
    top = jnp.maximum(prefix_peak, own_peak)
    from_prefix = jnp.exp(prefix_peak - top)
    from_own = jnp.exp(own_peak - top)
    numer = from_prefix[..., None] * prefix_sum + from_own[..., None] * own_sum
    denom = from_prefix * prefix_mass + from_own * own_mass
    return (numer / denom[..., None]).reshape(steps, rows_dev, heads * width).astype(jnp.bfloat16)


def solution(mesh):
    return jax.shard_map(
        local,
        mesh=mesh,
        in_specs=(
            P(None, ("rows", "prefix"), None, None),
            P(None, None, ("rows", "prefix"), None, None),
            P(None, ("rows", "prefix"), None, None, None),
            P(("rows", "prefix")),
            P(),
            P(None, "prefix", "rows", None, None),
            P("prefix", None),
            P("prefix", None),
            P("prefix"),
        ),
        out_specs=P(None, ("rows", "prefix"), None),
        check_vma=False,
    )
```

profile of v0, /device:TPU:1, one launch (start us, length us, event | category | flops | bytes accessed | tf_op | source)
XLA Modules:
  0.0 528.7 jit_solution(11824955011786561215)
XLA Ops:
  6.5 0.7 all-gather.2.cloned.1.call-update
  7.3 49.0 %all-gather.2.cloned.1.call-done = bf16[4,32,32,128]{3,2,0,1:T(8,128)(2,1)} async-done(((bf16[4,1,32,128]{3,2,0,1:T(8,128)(2,1)}), bf16[4,32,32,128]{3,2,0,1:T(8,128)(2,1)}) %all-gather.2.cloned.1.call-update) | async-done | bytes 1048592 | tf_op jit(solution)/shard_map/all_gather | solution.py:34
  56.2 2.9 copy.143
  59.2 4.0 all-to-all-start
  63.1 14.7 %all-to-all-done = bf16[4,32,32,128]{3,1,0,2:T(8,128)(2,1)S(1)} async-done(((bf16[4,32,32,128]{3,1,0,2:T(8,128)(2,1)}), bf16[4,32,32,128]{3,1,0,2:T(8,128)(2,1)S(1)}, u32[]{:S(2)}, u32[]{:S(2)}) %all-to-all-start) | async-done | bytes 1048608 | tf_op jit(solution)/shard_map/all_to_all | solution.py:35
  77.8 0.1 copy.144
  78.0 1.9 broadcast_in_dim.78.clone
  79.9 14.9 %while.15 = (s32[]{:T(128)}, f32[128,4,8]{0,2,1:T(8,128)S(1)}, f32[128,4,8]{0,2,1:T(8,128)S(1)}, f32[128,4,8,128]{3,1,2,0:T(4,128)}, s32[]{:T(128)}, /*index=5*/...) while((s32[]{:T(128)}, f32[128,4,8]{0,2,1:T(8,128)S(1)}, ...), condition=%wide.region_3.4_spmd.clone, body=%wide.region_0.3_spmd.clone.sunk | while | flops 276500480 | bytes 10944859 | solution.py:92
  80.5 0.6 constant_dynamic-slice_fusion.10
  81.8 0.1 constant_dynamic-slice_fusion.11
  83.7 0.6 dynamic_slice.70
  84.3 0.6 fusion.51
  84.9 1.2 fusion.52
  86.2 1.7 fusion.53
  87.9 0.6 convert_reduce_fusion.4
  88.5 0.1 reshape.333
  88.6 0.1 reshape.334
  88.8 0.7 dynamic_update_slice.17
  89.5 0.7 dynamic_update_slice.18
  90.2 1.0 constant_dynamic-slice_fusion.13
  91.2 1.9 fusion.55
  93.1 0.2 fusion.56
  93.3 0.8 copy_dynamic-update-slice_fusion.2
  94.8 249.1 %pmax.7 = f32[128,4,8]{0,2,1:T(8,128)S(1)} all-reduce(f32[128,4,8]{0,2,1:T(8,128)S(1)} %get-tuple-element.65), channel_id=1, replica_groups=mesh['rows'=4,'prefix'=32] {'prefix'}, use_global_device_ids=true, to_apply=%region_4.5 | all-reduce | flops 4096 | bytes 32768 | tf_op jit(solution)/shard_map/pmax | solution.py:95
  343.8 0.3 copy.155
  344.1 2.5 broadcast_multiply_fusion
  346.6 22.9 %all_to_all.72 = f32[128,4,8,128]{3,1,2,0:T(4,128)S(1)} all-to-all(f32[128,4,8,128]{3,1,2,0:T(4,128)S(1)} %broadcast_multiply_fusion), channel_id=1, replica_groups=mesh['rows'=4,'prefix'=32] {'rows'}, dimensions={0} | all-to-all | bytes 4194304 | tf_op jit(solution)/shard_map/all_to_all | solution.py:101
  369.5 0.2 copy.157
  369.7 1.6 copy.229
  372.2 0.4 fusion.39
  372.6 0.3 copy-done
  372.9 0.4 fusion.36
  373.3 0.5 fusion.38
  373.8 0.4 fusion.21
  374.2 0.2 convolution_add_fusion
  374.4 0.1 copy.164
  374.6 0.9 reshape.329
  375.4 3.3 all-to-all-start.3
  378.7 0.2 convert_reduce_fusion.1
  378.9 0.1 copy.146
  379.1 0.9 reshape.327
  379.9 2.9 all-to-all-done.3
  382.9 3.2 all-to-all-start.1
  386.1 0.1 convert_reduce_fusion.2
  386.2 0.1 copy.168
  386.3 0.1 copy.153
  386.4 0.6 dynamic-slice
  387.0 0.5 broadcast.52
  387.5 0.7 reduce.6
  388.2 0.3 reshape.330
  388.6 0.1 copy.166
  388.7 0.1 copy.167
  388.8 1.7 all-to-all-done.1
  390.5 0.7 reduce.7
  391.2 0.3 reshape.328
  391.5 0.1 copy.148
  391.7 0.2 dynamic-slice_reduce_fusion
  391.8 127.5 %all-reduce = f32[32,4,32]{2,1,0:T(4,128)S(1)} all-reduce(f32[32,4,32]{2,1,0:T(4,128)S(1)} %copy.167), channel_id=3, replica_groups=mesh['rows'=4,'prefix'=32] {'prefix'}, use_global_device_ids=true, to_apply=%region_8.9.clone | all-reduce | flops 4096 | bytes 32768
  519.3 0.6 fusion.30
  519.9 0.1 div.20
  520.1 0.1 mul.137
  520.2 0.1 mul.132
  520.3 0.9 transpose.64
  521.2 0.7 fusion.23
  (32 shorter events, 0.3 us)
Async XLA Ops:
  6.5 49.7 %all-gather.2.cloned.1.call-start = ((), (), s32[]{:S(2)}) async-start(), calls=%async_computation.5 | async-start | bytes 1081344 | tf_op jit(solution)/shard_map/all_gather | solution.py:34
  59.2 18.7 %all-to-all-start = ((bf16[4,32,32,128]{3,1,0,2:T(8,128)(2,1)}), bf16[4,32,32,128]{3,1,0,2:T(8,128)(2,1)S(1)}, u32[]{:S(2)}, u32[]{:S(2)}) async-start(bf16[4,32,32,128]{3,1,0,2:T(8,128)(2,1)} %copy.143), calls=%async_computation | async-start | bytes 2097152 | tf_op jit(solution)/shard_map/all_to_all | solution.py:35
  63.1 457.2 %reduce-scatter.2.cloned.1.call-start = ((), (), s32[]{:S(2)}) async-start(), calls=%async_computation.6 | async-start | bytes 2162688 | tf_op jit(solution)/shard_map/reduce_scatter | solution.py:106
  77.8 2.1 copy-start.3
  77.8 2.1 copy-start.4
  77.8 2.1 copy-start.5
  369.7 2.5 copy-start.1
  371.3 0.9 copy-start.2
  371.3 1.6 copy-start
  373.8 12.6 %copy-start.6 = (u32[128]{0:T(128)S(1)}, u32[128]{0:T(128)}, u32[]{:S(2)}) copy-start(u32[128]{0:T(128)} %constant.53) | copy-start | bytes 1540
  375.4 7.4 %all-to-all-start.3 = ((f32[4,1,1024]{2,1,0:T(1,128)}), f32[4,1,1024]{2,1,0:T(1,128)S(1)}, u32[]{:S(2)}, u32[]{:S(2)}) async-start(f32[4,1,1024]{2,1,0:T(1,128)} %reshape.329), calls=%async_computation.4 | async-start | bytes 32768 | tf_op jit(solution)/shard_map/all_to_all | solution.py:100
  382.9 7.6 %all-to-all-start.1 = ((f32[4,1,1024]{2,1,0:T(1,128)}), f32[4,1,1024]{2,1,0:T(1,128)S(1)}, u32[]{:S(2)}, u32[]{:S(2)}) async-start(f32[4,1,1024]{2,1,0:T(1,128)} %reshape.327), calls=%async_computation.1 | async-start | bytes 32768 | tf_op jit(solution)/shard_map/all_to_all | solution.py:102
Sparse Core Ops, SparseCore 0:
  9.6 46.5 all-gather.1
  371.5 79.4 reduce-scatter.1
where the time goes:
time: 535 us; the launch traced here: 529 us
  blocking collectives  399 us (75%)
  waiting for transfers between devices  69 us (13%)
  local copies, waits for them, and re-layouts  18.1 us (3%)
  between operations  14.4 us (3%)
  starting transfers between devices  10.5 us (2%)
  other arithmetic  8.2 us (2%)
    pmax x1, blocking collectives, local(): shared_peak = lax.pmax(peak_rows, 'prefix')  249 us
    unnamed x1, blocking collectives  127 us
    all_gather x1, waiting for transfers between devices, local(): gathered = lax.all_gather(queries, 'prefix', axis=1, tiled=True)  49 us
    all_to_all x1, blocking collectives, local(): lax.all_to_all(sum_rows, 'rows', split_axis=0, concat_axis=2, tiled=True)  22.9 us
    all_to_all x1, waiting for transfers between devices, local(): lax.all_to_all(gathered, 'rows', split_axis=2, concat_axis=1, tiled=True)  14.7 us
  transfers between devices with their start and end apart: 5, of which 4 were waited for; matrix products, arithmetic and copies ran while one was open for 2% of the time, Pallas kernels for 0%

commit v1 on v0

v1 whole, which is shorter than its diff:
```python
import functools
import math

import jax
import jax.numpy as jnp
from jax import lax
from jax.experimental import pallas as pl
from jax.experimental.pallas import tpu as pltpu
from jax.sharding import PartitionSpec as P

MESH = pl.DeviceIdType.MESH
SAMPLES = 16
masked_score = -1e30
exponent = 168.0 ** (-0.5) * math.log2(math.e)
f32 = jnp.float32
bf16 = jnp.bfloat16
NT = (((1,), (1,)), ((), ()))
NN = (((1,), (0,)), ((), ()))
UNROLL = 5


def iota(shape, dim):
    return lax.broadcasted_iota(jnp.int32, shape, dim)


def kernel(
    n_x,
    n_i,
    block_len,
    slots,
    prompt_ref,
    index_ref,
    count_ref,
    prefix_len_ref,
    suffix_len_ref,
    q_ref,
    new_ref,
    suffix_hbm,
    prefix_hbm,
    out_ref,
    kv,
    suf,
    q_own,
    q_x,
    q_src,
    q_all,
    q_prompt,
    own_s,
    own_acc,
    own_m,
    own_l,
    accs,
    ms,
    ls,
    acc_sel,
    m_sel,
    l_sel,
    part,
    part_in,
    stat,
    stat_in,
    fin,
    fin_in,
    kv_sem,
    suf_sem,
    x_send,
    x_recv,
    q_send,
    q_recv,
    part_send,
    part_recv,
    stat_send,
    stat_recv,
    fin_send,
    fin_recv,
):
    me_x = lax.axis_index("rows")
    me_i = lax.axis_index("prefix")
    kv_local = kv.shape[0]
    rows = q_ref.shape[0]

    suf_copy = pltpu.make_async_copy(suffix_hbm, suf, suf_sem)
    suf_copy.start()
    kv_copies = [
        pltpu.make_async_copy(prefix_hbm.at[:, :, k], kv.at[k], kv_sem.at[k])
        for k in range(kv_local)
    ]
    for copy in kv_copies:
        copy.start()

    def peer(d):
        return lax.rem(me_i + d, n_i)

    def mate(d):
        return lax.rem(me_x + d, n_x)

    barrier = pltpu.get_barrier_semaphore()

    def greet(d, carry):
        pl.semaphore_signal(barrier, inc=1, device_id=(me_x, peer(d)), device_id_type=MESH)
        return carry

    lax.fori_loop(1, n_i, greet, 0)
    for d in range(1, n_x):
        pl.semaphore_signal(barrier, inc=1, device_id=(mate(d), me_i), device_id_type=MESH)

    r = iota((rows, rows), 0)
    c = iota((rows, rows), 1)
    source = (lax.rem(r, 8) // 2) * 32 + (r // 8) * 2 + lax.rem(r, 2)
    order = jnp.where(c == source, 1.0, 0.0).astype(bf16)
    q_mine = lax.dot_general(order, q_ref[...], NN, preferred_element_type=f32).astype(bf16)
    q_own[...] = q_mine.reshape(n_x, 32, 128)
    stat[...] = jnp.zeros_like(stat)
    acc_sel[0] = jnp.zeros((rows, 128), f32)
    m_sel[0] = jnp.full((rows, 128), masked_score, f32)
    l_sel[0] = jnp.zeros((rows, 128), f32)

    pl.semaphore_wait(barrier, n_i - 1 + n_x - 1)

    def waiter(ref, send, recv):
        return pltpu.make_async_remote_copy(
            src_ref=ref,
            dst_ref=ref,
            send_sem=send,
            recv_sem=recv,
            device_id=(me_x, peer(1)),
            device_id_type=MESH,
        )

    for d in range(1, n_x):
        g = mate(d)
        pltpu.make_async_remote_copy(
            src_ref=q_own.at[g],
            dst_ref=q_x.at[me_x],
            send_sem=x_send,
            recv_sem=x_recv,
            device_id=(g, me_i),
            device_id_type=MESH,
        ).start()
    q_x[me_x] = q_own[me_x]
    waiter(q_x.at[pl.ds(0, n_x - 1)], x_send, x_recv).wait_recv()
    gathered = q_x[...].astype(f32).reshape(n_x, kv_local, 8, 128).transpose(1, 0, 2, 3)
    gathered = gathered.reshape(kv_local, n_x * 8, 128).astype(bf16)
    q_src[...] = gathered
    for k in range(kv_local):
        q_all[k, me_i] = gathered[k]
    for k in range(kv_local):

        def push_q(d, carry, k=k):
            pltpu.make_async_remote_copy(
                src_ref=q_src.at[k],
                dst_ref=q_all.at[k, me_i],
                send_sem=q_send.at[k],
                recv_sem=q_recv.at[k],
                device_id=(me_x, peer(d)),
                device_id_type=MESH,
            ).start()
            return carry

        lax.fori_loop(1, n_i, push_q, 0)

    suf_copy.wait()
    chunk = own_s.shape[2]
    chunks = own_s.shape[0]
    suffix_len = suffix_len_ref[0]
    row_head = iota((rows, 1), 0) // 8
    row_step = lax.rem(iota((rows, 1), 0), 8) // 2
    near = lax.dot_general(q_mine, new_ref[0], NT, preferred_element_type=f32)
    lane = iota((1, near.shape[1]), 1)
    near_live = (lax.rem(lane, 16) == row_head) & (lane // 16 <= row_step)
    near = jnp.where(near_live, near, masked_score)
    lane = iota((1, chunk), 1)
    same_head = lax.rem(lane, 16) == row_head

    def far_scores(n, peak):
        s = lax.dot_general(
            q_mine, suf[0, pl.ds(n * chunk, chunk)], NT, preferred_element_type=f32
        )
        live = same_head & (n * (chunk // 16) + lane // 16 < suffix_len)
        s = jnp.where(live, s, masked_score)
        own_s[n] = s
        return jnp.maximum(peak, jnp.max(s, axis=1, keepdims=True))

    own_peak = lax.fori_loop(0, chunks, far_scores, jnp.max(near, axis=1, keepdims=True))
    near_w = jnp.exp2((near - own_peak) * exponent).astype(bf16)
    near_sum = lax.dot_general(near_w, new_ref[1], NN, preferred_element_type=f32)
    near_mass = jnp.sum(near_w.astype(f32), axis=1, keepdims=True)
    ones = jnp.ones((chunk, 128), bf16)

    def far_sums(n, carry):
        total, mass = carry
        w = jnp.exp2((own_s[n] - own_peak) * exponent).astype(bf16)
        values = jnp.concatenate([suf[1, pl.ds(n * chunk, chunk)], ones], axis=1)
        both = lax.dot_general(w, values, NN, preferred_element_type=f32)
        return total + both[:, :128], mass + both[:, 128:]

    total, mass = lax.fori_loop(
        0, chunks, far_sums, (near_sum, jnp.broadcast_to(near_mass, (rows, 128)))
    )
    own_acc[...] = total
    own_l[...] = mass
    own_m[...] = jnp.broadcast_to(own_peak, (rows, 128))

    count = count_ref[0]
    prompt_a = prompt_ref[0, 0]
    prompt_b = prompt_ref[0, jnp.maximum(count - 1, 0)]
    column = iota((1, block_len), 1)
    ones = jnp.ones((block_len, 128), bf16)
    lane = iota((1, 1, 128), 2)

    def pick(p):
        return jnp.where(prompt_a == p, 1, jnp.where(prompt_b == p, 2, 0))

    for k in range(kv_local):
        waiter(q_all.at[k, pl.ds(0, n_i - 1)], q_send.at[k], q_recv.at[k]).wait_recv()
        for half in range(2):
            v = q_all[k, pl.ds(half * SAMPLES, SAMPLES)].astype(f32)
            v = v.reshape(SAMPLES, n_x, 8, 128)
            for x in range(n_x):
                q_prompt[2 * x + half] = v[:, x].reshape(rows, 128).astype(bf16)
        kv_copies[k].wait()

        def visit(step, carry, k=k):
            for u in range(UNROLL):
                j = step * UNROLL + u
                prompt = prompt_ref[0, j]
                live = prefix_len_ref[prompt] - index_ref[0, j] * block_len
                live = jnp.where(j < count, live, 0)
                s = lax.dot_general(
                    q_prompt[prompt], kv[k, 0, j], NT, preferred_element_type=f32
                )
                s = jnp.where(column < live, s, masked_score)
                m = jnp.max(s, axis=1, keepdims=True)
                w = jnp.exp2((s - m) * exponent).astype(bf16)
                values = jnp.concatenate([kv[k, 1, j], ones], axis=1)
                both = lax.dot_general(w, values, NN, preferred_element_type=f32)
                accs[j] = both[:, :128]
                ls[j] = both[:, 128:]
                ms[j] = jnp.broadcast_to(m, (rows, 128))
            return carry

        lax.fori_loop(0, slots // UNROLL, visit, 0)

        for place, prompt in ((1, prompt_a), (2, prompt_b)):
            outside = [jnp.where(prompt_ref[0, j] == prompt, 0.0, masked_score) for j in range(slots)]
            peak = ms[0] + outside[0]
            for j in range(1, slots):
                peak = jnp.maximum(peak, ms[j] + outside[j])
            total = jnp.zeros((rows, 128), f32)
            mass = jnp.zeros((rows, 128), f32)
            for j in range(slots):
                take = jnp.exp2((ms[j] + outside[j] - peak) * exponent)
                total = total + take * accs[j]
                mass = mass + take * ls[j]
            acc_sel[place] = total
            m_sel[place] = peak
            l_sel[place] = mass

        for half in range(2):
            span = pl.ds(half * SAMPLES, SAMPLES)
            st = stat[span]
            parts = []
            for x in range(n_x):
                which = pick(2 * x + half)
                parts.append(acc_sel[which].reshape(SAMPLES, 1, 8, 128))
                at = x * 32 + k * 8
                st = jnp.where(lane == at, m_sel[which].reshape(SAMPLES, 8, 128), st)
                st = jnp.where(lane == at + 1, l_sel[which].reshape(SAMPLES, 8, 128), st)
            stat[span] = st
            block = jnp.concatenate(parts, axis=1).reshape(SAMPLES, n_x * 8, 128)
            part[k, span] = block.astype(bf16)

        def push_part(d, carry, k=k):
            to = peer(d)
            pltpu.make_async_remote_copy(
                src_ref=part.at[k, to],
                dst_ref=part_in.at[k, me_i],
                send_sem=part_send.at[k],
                recv_sem=part_recv.at[k],
                device_id=(me_x, to),
                device_id_type=MESH,
            ).start()
            return carry

        def push_stat(d, carry):
            to = peer(d)
            pltpu.make_async_remote_copy(
                src_ref=stat.at[to],
                dst_ref=stat_in.at[me_i],
                send_sem=stat_send,
                recv_sem=stat_recv,
                device_id=(me_x, to),
                device_id_type=MESH,
            ).start()
            return carry

        if k == kv_local - 1:
            lax.fori_loop(1, n_i, push_stat, 0)
        lax.fori_loop(1, n_i, push_part, 0)
        part_in[k, me_i] = part[k, me_i]
    stat_in[me_i] = stat[me_i]

    stat_wait = waiter(stat_in.at[pl.ds(0, n_i - 1)], stat_send, stat_recv)
    stat_wait.wait_recv()
    st = stat_in[...]
    peak = jnp.max(st, axis=0)
    factor = jnp.exp2((st - peak) * exponent)
    mass_at = pltpu.roll(st.reshape(n_i * 8, 128), 127, 1).reshape(n_i, 8, 128)
    mass = jnp.sum(factor * mass_at, axis=0)
    stat_in[...] = factor
    part_waits = []
    for k in range(kv_local):
        part_wait = waiter(part_in.at[k, pl.ds(0, n_i - 1)], part_send.at[k], part_recv.at[k])
        part_wait.wait_recv()
        part_waits.append(part_wait)

    def add_owner(o, carry):
        carry = list(carry)
        f = stat_in[o]
        for k in range(kv_local):
            v = part_in[k, o].astype(f32)
            for x in range(n_x):
                at = x * 32 + k * 8
                n = k * n_x + x
                carry[n] = carry[n] + f[:, at : at + 1] * v[x * 8 : x * 8 + 8]
        return tuple(carry)

    sums = lax.fori_loop(
        0, n_i, add_owner, tuple(jnp.zeros((8, 128), f32) for _ in range(kv_local * n_x)), unroll=4
    )
    lane = iota((1, 128), 1)
    both = jnp.where(lax.rem(lane, 8) == 1, pltpu.roll(mass, 1, 1), peak)
    for x in range(n_x):
        for k in range(kv_local):
            fin[x, k * 8 : k * 8 + 8] = sums[k * n_x + x]
        fin[x, kv_local * 8 : kv_local * 8 + 8] = pltpu.roll(both, (128 - 32 * x) % 128, 1) if x else both
    for d in range(1, n_x):
        x = mate(d)
        pltpu.make_async_remote_copy(
            src_ref=fin.at[x],
            dst_ref=fin_in.at[me_x],
            send_sem=fin_send,
            recv_sem=fin_recv,
            device_id=(x, me_i),
            device_id_type=MESH,
        ).start()
    fin_in[me_x] = fin[me_x]
    fin_wait = waiter(fin_in.at[pl.ds(0, n_x - 1)], fin_send, fin_recv)
    fin_wait.wait_recv()

    result = []
    for g in range(n_x):
        st = fin_in[g, kv_local * 8 : kv_local * 8 + 8]
        for k in range(kv_local):
            at = (g * kv_local + k) * 8
            span = slice(at, at + 8)
            prefix_peak = st[:, k * 8 : k * 8 + 1]
            prefix_mass = st[:, k * 8 + 1 : k * 8 + 2]
            mine = own_m[span, :]
            top = jnp.maximum(prefix_peak, mine)
            from_prefix = jnp.exp2((prefix_peak - top) * exponent)
            from_own = jnp.exp2((mine - top) * exponent)
            numer = from_prefix * fin_in[g, k * 8 : k * 8 + 8] + from_own * own_acc[span, :]
            denom = from_prefix * prefix_mass + from_own * own_l[span, :]
            result.append(numer / denom)
    result = jnp.concatenate(result, axis=0).astype(bf16)
    source = lax.rem(r, 32) // 2 * 8 + (r // 32) * 2 + lax.rem(r, 2)
    order = jnp.where(c == source, 1.0, 0.0).astype(bf16)
    out_ref[...] = lax.dot_general(order, result, NN, preferred_element_type=f32).astype(bf16)

    waiter(q_x.at[pl.ds(0, n_x - 1)], x_send, x_recv).wait_send()
    for k in range(kv_local):
        waiter(q_all.at[k, pl.ds(0, n_i - 1)], q_send.at[k], q_recv.at[k]).wait_send()
        part_waits[k].wait_send()
    stat_wait.wait_send()
    fin_wait.wait_send()


def local(
    n_x,
    n_i,
    queries,
    new_kv,
    suffix_kv,
    suffix_len,
    prefix_len,
    prefix_kv,
    block_prompt,
    block_index,
    block_count,
):
    steps, rows_dev, heads, width = queries.shape
    slots, kv_local, block_len = prefix_kv.shape[1:4]
    rows = steps * heads
    q = queries.reshape(rows, width)
    new = new_kv.reshape(2, -1, width)
    suffix = suffix_kv.reshape(2, -1, width)
    keys = suffix.shape[1]
    chunk = 1024
    smem = pl.BlockSpec(memory_space=pltpu.SMEM)
    vmem = pl.BlockSpec(memory_space=pltpu.VMEM)
    hbm = pl.BlockSpec(memory_space=pl.ANY)
    dma = pltpu.SemaphoreType.DMA
    out = pl.pallas_call(
        functools.partial(kernel, n_x, n_i, block_len, slots),
        out_shape=jax.ShapeDtypeStruct((rows, width), bf16),
        in_specs=[smem] * 5 + [vmem, vmem, hbm, hbm],
        out_specs=vmem,
        scratch_shapes=[
            pltpu.VMEM((kv_local, 2, slots, block_len, width), bf16),
            pltpu.VMEM((2, keys, width), bf16),
            pltpu.VMEM((n_x, 32, width), bf16),
            pltpu.VMEM((n_x, 32, width), bf16),
            pltpu.VMEM((kv_local, n_x * 8, width), bf16),
            pltpu.VMEM((kv_local, n_i, n_x * 8, width), bf16),
            pltpu.VMEM((8, rows, width), bf16),
            pltpu.VMEM((keys // chunk, rows, chunk), f32),
            pltpu.VMEM((rows, width), f32),
            pltpu.VMEM((rows, width), f32),
            pltpu.VMEM((rows, width), f32),
            pltpu.VMEM((slots, rows, width), f32),
            pltpu.VMEM((slots, rows, width), f32),
            pltpu.VMEM((slots, rows, width), f32),
            pltpu.VMEM((3, rows, width), f32),
            pltpu.VMEM((3, rows, width), f32),
            pltpu.VMEM((3, rows, width), f32),
            pltpu.VMEM((kv_local, n_i, n_x * 8, width), bf16),
            pltpu.VMEM((kv_local, n_i, n_x * 8, width), bf16),
            pltpu.VMEM((n_i, 8, 128), f32),
            pltpu.VMEM((n_i, 8, 128), f32),
            pltpu.VMEM((n_x, (kv_local + 1) * 8, width), f32),
            pltpu.VMEM((n_x, (kv_local + 1) * 8, width), f32),
            dma((kv_local,)),
            dma,
            dma,
            dma,
            dma((kv_local,)),
            dma((kv_local,)),
            dma((kv_local,)),
            dma((kv_local,)),
            dma,
            dma,
            dma,
            dma,
        ],
        compiler_params=pltpu.CompilerParams(
            collective_id=0, has_side_effects=True, vmem_limit_bytes=60 << 20
        ),
        name="decode_attention",
    )(block_prompt, block_index, block_count, prefix_len, suffix_len, q, new, suffix, prefix_kv)
    return out.reshape(steps, rows_dev, heads * width)


def solution(mesh):
    return jax.shard_map(
        functools.partial(local, mesh.shape["rows"], mesh.shape["prefix"]),
        mesh=mesh,
        in_specs=(
            P(None, ("rows", "prefix"), None, None),
            P(None, None, ("rows", "prefix"), None, None),
            P(None, ("rows", "prefix"), None, None, None),
            P(("rows", "prefix")),
            P(),
            P(None, "prefix", "rows", None, None),
            P("prefix", None),
            P("prefix", None),
            P("prefix"),
        ),
        out_specs=P(None, ("rows", "prefix"), None),
        check_vma=False,
    )
```

time: 535 us -> 48.4 us (0.09); the launches traced: 529 us -> 48.1 us
  blocking collectives: 399 us -> 0 us
  waiting for transfers between devices: 69 us -> 0 us
  Pallas kernels: 0 us -> 45.4 us
  local copies, waits for them, and re-layouts: 18.1 us -> 1.39 us
  between operations: 14.4 us -> 1.3 us
  starting transfers between devices: 10.5 us -> 0 us
  other arithmetic: 8.2 us -> 0 us
    pmax x1 -> x0, blocking collectives: 249 us -> none  [local(): shared_peak = lax.pmax(peak_rows, 'prefix')]
    unnamed x1 -> x0, blocking collectives: 127 us -> none
    all_gather x1 -> x0, waiting for transfers between devices: 49 us -> none  [local(): gathered = lax.all_gather(queries, 'prefix', axis=1, tiled=True)]
    pallas_call x0 -> x1, Pallas kernels: none -> 45.4 us  [local(): pl.pallas_call(functools.partial(kernel, n_x, n_i, block_len, slots), out...]
    all_to_all x1 -> x0, blocking collectives: 22.9 us -> none  [local(): lax.all_to_all(sum_rows, 'rows', split_axis=0, concat_axis=2, tiled=True)]
    all_to_all x3 -> x0, waiting for transfers between devices: 19.3 us -> none  [the longest x1 14.7 us: local(): lax.all_to_all(gathered, 'rows', split_axis=2, concat_axis=1, tiled=True)]
    all_to_all x3 -> x0, starting transfers between devices: 10.5 us -> none  [the longest x1 3.97 us: local(): lax.all_to_all(gathered, 'rows', split_axis=2, concat_axis=1, tiled=True)]
  transfers between devices with their start and end apart: 5 -> 0, of which waited for: 4 -> 0; matrix products, arithmetic and copies ran while one was open for 2% -> 0% of each run, Pallas kernels for 0% -> 0%
where the time goes in v1:
time: 48.4 us; the launch traced here: 48.1 us
  Pallas kernels  45.4 us (94%)
  local copies, waits for them, and re-layouts  1.39 us (3%)
  between operations  1.3 us (3%)
    pallas_call x1, Pallas kernels, local(): pl.pallas_call(functools.partial(kernel, n_x, n_i, block_len, slots), out...  45.4 us
    reshape x1, local copies, waits for them, and re-layouts, local(): return out.reshape(steps, rows_dev, heads * width)  1.39 us

profile of v1, /device:TPU:1, one launch (start us, length us, event | category | flops | bytes accessed | tf_op | source)
XLA Modules:
  0.0 48.1 jit_solution(1153352689037419567)
XLA Ops:
  1.3 45.4 %decode_attention.1 = bf16[128,128]{1,0:T(8,128)(2,1)} custom-call(s32[1,10]{1,0:T(1,128)} %prompt_ref.1, s32[1,10]{1,0:T(1,128)} %index_ref.1, s32[1]{0:T(128)S(6)} %copy.11.count_ref, s32[8]{0:T(128)} %prefix_len_ref.1, s32[1]{0:T(128)S(6)} %copy.10.suffix_len_ref, bf16[128,128]{1,0:T(8,128)(2,1)} %bitcast.4, bf16[2,64,128]{2,1,0:T(8,128)(2,1)} %bitcast.5, ...), custom_call_target="tpu_custom_call" | custom-call | tf_op jit(solution)/shard_map/decode_attention/pallas_call | solution.py:404
  46.7 1.4 %reshape.15 = bf16[4,1,4096]{2,0,1:T(4,128)(2,1)} reshape(bf16[128,128]{1,0:T(8,128)(2,1)} %decode_attention.1) | data formatting | bytes 65536 | tf_op jit(solution)/shard_map/reshape | solution.py:451

commit v2 on v1

v2 whole, which is shorter than its diff:
```python
import functools
import math

import jax
import jax.numpy as jnp
from jax import lax
from jax.experimental import pallas as pl
from jax.experimental.pallas import tpu as pltpu
from jax.sharding import PartitionSpec as P

MESH = pl.DeviceIdType.MESH
SAMPLES = 16
masked_score = -1e30
exponent = 168.0 ** (-0.5) * math.log2(math.e)
f32 = jnp.float32
bf16 = jnp.bfloat16
NT = (((1,), (1,)), ((), ()))
NN = (((1,), (0,)), ((), ()))
X_ORDER = (0, 1, 3, 2)


def iota(shape, dim):
    return lax.broadcasted_iota(jnp.int32, shape, dim)


def kernel(
    n_x,
    n_i,
    block_len,
    slots,
    prompt_hbm,
    index_hbm,
    count_hbm,
    prefix_len_hbm,
    suffix_len_hbm,
    q_hbm,
    new_hbm,
    suffix_hbm,
    prefix_hbm,
    out_ref,
    prompt_ref,
    index_ref,
    count_ref,
    prefix_len_ref,
    suffix_len_ref,
    q_ref,
    new_ref,
    kv,
    suf,
    q_own,
    q_all,
    q_prompt,
    own_s,
    own_acc,
    own_m,
    own_l,
    m_sel,
    packed,
    tag,
    tag_in,
    part,
    part_in,
    stat,
    stat_in,
    fin,
    fin_in,
    int_sem,
    small_sem,
    kv_sem,
    suf_sem,
    q_send,
    q_recv,
    forward_send,
    forward_recv,
    tag_send,
    tag_recv,
    part_send,
    part_recv,
    stat_send,
    stat_recv,
    fin_send,
    fin_recv,
):
    me_x = lax.axis_index("rows")
    me_i = lax.axis_index("prefix")
    me_j = me_i // 2
    me_c = lax.rem(me_i, 2)
    other_c = 1 - me_c
    sibling = (me_x, me_j * 2 + other_c)
    n_j = n_i // 2
    kv_local = kv.shape[0]
    rows = q_ref.shape[0]
    half_j = SAMPLES // 2
    lane = iota((1, 128), 1)
    pairs = kv_local // 2

    def peer(d):
        return lax.rem(me_i + d, n_i)

    def sample(i):
        return lax.rem(i, 2) * half_j + lax.rem(i, SAMPLES) // 2

    def on_core(d):
        return lax.rem(me_j + d, n_j) * 2 + me_c

    def mate(d):
        return lax.rem(me_x + d, n_x)

    barrier = pltpu.get_barrier_semaphore()

    def greet_other(j, carry):
        pl.semaphore_signal(
            barrier, inc=1, device_id=(me_x, j * 2 + other_c), device_id_type=MESH
        )
        return carry

    lax.fori_loop(0, n_j, greet_other, 0)
    for dx in range(n_x):

        def greet(d, carry, dx=dx):
            pl.semaphore_signal(
                barrier, inc=1, device_id=(mate(dx), on_core(d)), device_id_type=MESH
            )
            return carry

        lax.fori_loop(1 if dx == 0 else 0, n_j, greet, 0)

    small_copies = [
        pltpu.make_async_copy(q_hbm, q_ref, small_sem.at[0]),
        pltpu.make_async_copy(new_hbm, new_ref, small_sem.at[1]),
    ]
    int_copies = [
        pltpu.make_async_copy(src, dst, int_sem.at[n])
        for n, (src, dst) in enumerate(
            (
                (prompt_hbm, prompt_ref),
                (index_hbm, index_ref),
                (count_hbm, count_ref),
                (prefix_len_hbm, prefix_len_ref),
                (suffix_len_hbm, suffix_len_ref),
            )
        )
    ]
    suf_copy = pltpu.make_async_copy(suffix_hbm, suf, suf_sem)
    kv_copies = [
        pltpu.make_async_copy(prefix_hbm.at[:, :, k], kv.at[k], kv_sem.at[k])
        for k in range(kv_local)
    ]
    for copy in small_copies + int_copies + [suf_copy]:
        copy.start()

    r = iota((rows, rows), 0)
    c = iota((rows, rows), 1)
    source = lax.rem(r, 4) * 32 + (r // 8) * 2 + lax.rem(r // 4, 2)
    order = jnp.where(c == source, 1.0, 0.0).astype(bf16)
    small_copies[0].wait()
    q_mine = lax.dot_general(order, q_ref[...], NN, preferred_element_type=f32).astype(bf16)
    q_own[...] = q_mine.reshape(n_x, pairs, 16, 128)
    for pair in range(pairs):
        q_all[pair, me_c, me_x, me_j] = q_own[me_x, pair]
    packed[...] = jnp.zeros_like(packed)

    pl.semaphore_wait(barrier, n_x * n_j - 1 + n_j)

    def waiter(ref, send, recv):
        return pltpu.make_async_remote_copy(
            src_ref=ref,
            dst_ref=ref,
            send_sem=send,
            recv_sem=recv,
            device_id=sibling,
            device_id_type=MESH,
        )

    def push(src, dst, send, recv, to):
        pltpu.make_async_remote_copy(
            src_ref=src,
            dst_ref=dst,
            send_sem=send,
            recv_sem=recv,
            device_id=to,
            device_id_type=MESH,
        ).start()

    for pair in range(pairs):
        for dx in X_ORDER:

            def push_q(d, carry, pair=pair, dx=dx):
                x = mate(dx)
                push(
                    q_own.at[x, pair],
                    q_all.at[pair, me_c, me_x, me_j],
                    q_send.at[pair, dx],
                    q_recv.at[pair, dx],
                    (x, on_core(d)),
                )
                return carry

            lax.fori_loop(1 if dx == 0 else 0, n_j, push_q, 0)
    for copy in kv_copies:
        copy.start()

    def q_wait(pair, dx):
        chunks = q_all.at[pair, me_c, 0, pl.ds(0, n_j - 1 if dx == 0 else n_j)]
        return waiter(chunks, q_send.at[pair, dx], q_recv.at[pair, dx])

    for copy in small_copies[1:] + int_copies + [suf_copy]:
        copy.wait()
    count = count_ref[0]
    prompt_a = prompt_ref[0, 0]
    prompt_b = prompt_ref[0, jnp.maximum(count - 1, 0)]
    base = lax.rem(me_i, 8) * 16
    in_first = (lane >= base) & (lane < base + 8)
    in_second = (lane >= base + 8) & (lane < base + 16)
    tag_a = prompt_a.astype(f32)
    tag_b = jnp.where(prompt_b == prompt_a, -1, prompt_b).astype(f32)
    tags = jnp.where(in_first, tag_a, jnp.where(in_second, tag_b, 0.0))
    tag[...] = jnp.broadcast_to(tags, (8, 128))
    tag_in[me_i] = tag[...]

    def push_tag(d, carry):
        push(tag, tag_in.at[me_i], tag_send, tag_recv, (me_x, peer(d)))
        return carry

    lax.fori_loop(1, n_i, push_tag, 0)
    chunk = own_s.shape[2]
    chunks = own_s.shape[0]
    suffix_len = suffix_len_ref[0]
    row_head = iota((rows, 1), 0) // 8
    row_step = lax.rem(iota((rows, 1), 0), 4)
    near = lax.dot_general(q_mine, new_ref[0], NT, preferred_element_type=f32)
    key = iota((1, near.shape[1]), 1)
    near_live = (lax.rem(key, 16) == row_head) & (key // 16 <= row_step)
    near = jnp.where(near_live, near, masked_score)
    key = iota((1, chunk), 1)
    same_head = lax.rem(key, 16) == row_head

    def far_scores(n, peak):
        s = lax.dot_general(
            q_mine, suf[0, pl.ds(n * chunk, chunk)], NT, preferred_element_type=f32
        )
        live = same_head & (n * (chunk // 16) + key // 16 < suffix_len)
        s = jnp.where(live, s, masked_score)
        own_s[n] = s
        return jnp.maximum(peak, jnp.max(s, axis=1, keepdims=True))

    own_peak = lax.fori_loop(0, chunks, far_scores, jnp.max(near, axis=1, keepdims=True))
    near_w = jnp.exp2((near - own_peak) * exponent).astype(bf16)
    near_sum = lax.dot_general(near_w, new_ref[1], NN, preferred_element_type=f32)
    near_mass = jnp.sum(near_w.astype(f32), axis=1, keepdims=True)
    ones = jnp.ones((chunk, 128), bf16)

    def far_sums(n, carry):
        total, mass = carry
        w = jnp.exp2((own_s[n] - own_peak) * exponent).astype(bf16)
        values = jnp.concatenate([suf[1, pl.ds(n * chunk, chunk)], ones], axis=1)
        both = lax.dot_general(w, values, NN, preferred_element_type=f32)
        return total + both[:, :128], mass + both[:, 128:]

    total, mass = lax.fori_loop(
        0, chunks, far_sums, (near_sum, jnp.broadcast_to(near_mass, (rows, 128)))
    )
    own_acc[...] = total
    own_l[...] = mass
    own_m[...] = jnp.broadcast_to(own_peak, (rows, 128))

    column = iota((1, block_len), 1)
    ones = jnp.ones((block_len, 128), bf16)
    in_a = [jnp.where(prompt_ref[0, j] == prompt_a, 1, 0) for j in range(slots)]
    outside_a = outside_b = jnp.full((1, 128), masked_score, f32)
    for j in range(slots):
        inside = jnp.where(prompt_ref[0, j] == prompt_a, 0.0, masked_score)
        outside_a = jnp.where(lane == j, inside, outside_a)
        inside = jnp.where(prompt_ref[0, j] == prompt_b, 0.0, masked_score)
        outside_b = jnp.where(lane == j, inside, outside_b)

    def forward_q(pair):
        for dx in X_ORDER:
            q_wait(pair, dx).wait_recv()
            mine = q_all.at[pair, me_c, lax.rem(me_x + n_x - dx, n_x)]
            push(mine, mine, forward_send.at[pair, dx], forward_recv.at[pair, dx], sibling)

    def push_part(k):
        def one(d, carry):
            to = peer(d)
            push(
                part.at[k, sample(to)],
                part_in.at[k, me_i],
                part_send.at[k],
                part_recv.at[k],
                (me_x, to),
            )
            return carry

        lax.fori_loop(1, n_i, one, 0)
        part_in[k, me_i] = part[k, sample(me_i)]

    def push_stat(d, carry):
        to = peer(d)
        push(stat.at[sample(to)], stat_in.at[me_i], stat_send, stat_recv, (me_x, to))
        return carry

    forward_q(0)
    for k in range(kv_local):
        pair = k // 2
        if k % 2 == 0:
            for dx in X_ORDER:
                waiter(
                    q_all.at[pair, me_c, 0], forward_send.at[pair, dx], forward_recv.at[pair, dx]
                ).wait_recv()
            for half in range(2):
                for x in range(n_x):
                    v = q_all[pair, :, x, pl.ds(half * half_j, half_j)].astype(f32)
                    v = v.reshape(SAMPLES, 2, 8, 128)
                    for n in range(2):
                        q_prompt[n, 2 * x + half] = v[:, n].reshape(rows, 128).astype(bf16)
        elif pair + 1 < pairs:
            forward_q(pair + 1)
        kv_copies[k].wait()

        accs, ms = [], []
        peaks = jnp.full((rows, 128), masked_score, f32)
        masses = jnp.zeros((rows, 128), f32)
        for j in range(slots):
            prompt = prompt_ref[0, j]
            live = prefix_len_ref[prompt] - index_ref[0, j] * block_len
            live = jnp.where(j < count, live, 0)
            s = lax.dot_general(
                q_prompt[k % 2, prompt], kv[k, 0, j], NT, preferred_element_type=f32
            )
            s = jnp.where(column < live, s, masked_score)
            m = jnp.max(s, axis=1, keepdims=True)
            w = jnp.exp2((s - m) * exponent).astype(bf16)
            values = jnp.concatenate([kv[k, 1, j], ones], axis=1)
            both = lax.dot_general(w, values, NN, preferred_element_type=f32)
            accs.append(both[:, :128])
            ms.append(m)
            peaks = jnp.where(lane == j, m, peaks)
            masses = jnp.where(lane == j, both[:, 128:], masses)

        pack = packed[...]
        for place, outside in ((1, outside_a), (2, outside_b)):
            shifted = peaks + outside
            peak = jnp.max(shifted, axis=1, keepdims=True)
            take = jnp.exp2((shifted - peak) * exponent)
            mass = jnp.sum(take * masses, axis=1, keepdims=True)
            m_sel[place] = jnp.broadcast_to(peak, (rows, 128))
            at = (place - 1) * 8 + k * 2
            pack = jnp.where(lane == at, peak, jnp.where(lane == at + 1, mass, pack))
        packed[...] = pack
        total_a = total_b = jnp.zeros((rows, 128), f32)
        for j in range(slots):
            take = jnp.exp2((ms[j] - m_sel[2 - in_a[j]]) * exponent)
            taken = take * accs[j]
            total_a = total_a + jnp.where(in_a[j] == 1, taken, 0.0)
            total_b = total_b + jnp.where(in_a[j] == 1, 0.0, taken)
        parts = [t.reshape(SAMPLES, 8, 128) for t in (total_a, total_b)]
        part[k] = jnp.concatenate(parts, axis=1).astype(bf16)
        push_part(k)

    turned = packed[...].T
    first = pltpu.roll(turned[:8], base, 1)
    second = pltpu.roll(turned[8:16], base + 8, 1)
    for n in range(SAMPLES):
        shift = (128 - 8 * n) % 128
        one, two = (pltpu.roll(a, shift, 1) if shift else a for a in (first, second))
        stat[n] = jnp.where(in_first, one, jnp.where(in_second, two, 0.0))
    lax.fori_loop(1, n_i, push_stat, 0)
    stat_in[me_i] = stat[sample(me_i)]

    tag_wait = waiter(tag_in.at[pl.ds(0, n_i - 1)], tag_send, tag_recv)
    tag_wait.wait_recv()
    part_waits = [
        waiter(part_in.at[k, pl.ds(0, n_i - 1)], part_send.at[k], part_recv.at[k])
        for k in range(kv_local)
    ]
    stat_wait = waiter(stat_in.at[pl.ds(0, n_i - 1)], stat_send, stat_recv)

    def side_by_side(ref):
        groups = [functools.reduce(jnp.add, [ref[g * 8 + n] for n in range(8)]) for g in range(n_i // 8)]
        return jnp.concatenate(groups, axis=1)

    key = iota((1, n_i * 16), 1)
    row = iota((n_x * 8, 1), 0)
    prompt = (row // 8 * 2 + lax.rem(me_i // SAMPLES, 2)).astype(f32)
    same = (lax.rem(key, 8) == lax.rem(row, 8)) & (side_by_side(tag_in)[:1] == prompt)
    stat_wait.wait_recv()
    st = side_by_side(stat_in)
    tile = jnp.zeros((n_x * 8, 128), f32)
    for k in range(kv_local):
        part_waits[k].wait_recv()
        peaks = jnp.where(same, st[k * 2 : k * 2 + 1], masked_score)
        peak = jnp.max(peaks, axis=1, keepdims=True)
        factor = jnp.where(same, jnp.exp2((peaks - peak) * exponent), 0.0)
        mass = jnp.sum(factor * st[k * 2 + 1 : k * 2 + 2], axis=1, keepdims=True)
        high = factor.astype(bf16)
        low = (factor - high.astype(f32)).astype(bf16)
        parts = part_in[k].reshape(n_i * 16, 128)
        total = lax.dot_general(high, parts, NN, preferred_element_type=f32)
        total = total + lax.dot_general(low, parts, NN, preferred_element_type=f32)
        fin[:, k * 8 : k * 8 + 8] = total.reshape(n_x, 8, 128)
        tile = jnp.where(lane == k * 2, peak, jnp.where(lane == k * 2 + 1, mass, tile))
    fin[:, kv_local * 8 : kv_local * 8 + 8] = tile.reshape(n_x, 8, 128)
    for d in range(1, n_x):
        x = mate(d)
        push(fin.at[x], fin_in.at[me_x], fin_send, fin_recv, (x, me_i))
    fin_in[me_x] = fin[me_x]
    fin_wait = waiter(fin_in.at[pl.ds(0, n_x - 1)], fin_send, fin_recv)
    fin_wait.wait_recv()

    for g in range(n_x):
        st = fin_in[g, kv_local * 8 : kv_local * 8 + 8]
        for k in range(kv_local):
            at = (g * kv_local + k) * 8
            span = slice(at, at + 8)
            prefix_peak = st[:, k * 2 : k * 2 + 1]
            prefix_mass = st[:, k * 2 + 1 : k * 2 + 2]
            peak = own_m[span, :]
            top = jnp.maximum(prefix_peak, peak)
            from_prefix = jnp.exp2((prefix_peak - top) * exponent)
            from_own = jnp.exp2((peak - top) * exponent)
            numer = from_prefix * fin_in[g, k * 8 : k * 8 + 8] + from_own * own_acc[span, :]
            denom = from_prefix * prefix_mass + from_own * own_l[span, :]
            result = (numer / denom).astype(bf16)
            for n in range(2):
                head = (g * kv_local + k) * 2 + n
                out_ref[:, head * 128 : head * 128 + 128] = result[n * 4 : n * 4 + 4]

    for pair in range(pairs):
        for dx in range(n_x):
            q_wait(pair, dx).wait_send()
            waiter(
                q_all.at[pair, me_c, 0], forward_send.at[pair, dx], forward_recv.at[pair, dx]
            ).wait_send()
    for k in range(kv_local):
        part_waits[k].wait_send()
    tag_wait.wait_send()
    stat_wait.wait_send()
    fin_wait.wait_send()


def local(
    n_x,
    n_i,
    queries,
    new_kv,
    suffix_kv,
    suffix_len,
    prefix_len,
    prefix_kv,
    block_prompt,
    block_index,
    block_count,
):
    steps, rows_dev, heads, width = queries.shape
    slots, kv_local, block_len = prefix_kv.shape[1:4]
    rows = steps * heads
    n_j = n_i // 2
    q = queries.reshape(rows, width)
    new = new_kv.reshape(2, -1, width)
    suffix = suffix_kv.reshape(2, -1, width)
    keys = suffix.shape[1]
    chunk = 1024
    ints = (block_prompt, block_index, block_count, prefix_len, suffix_len)
    hbm = pl.BlockSpec(memory_space=pl.ANY)
    dma = pltpu.SemaphoreType.DMA
    per_row = pltpu.VMEM((rows, width), f32)
    out = pl.pallas_call(
        functools.partial(kernel, n_x, n_i, block_len, slots),
        out_shape=jax.ShapeDtypeStruct((steps, heads * width), bf16),
        in_specs=[hbm] * 9,
        out_specs=pl.BlockSpec(memory_space=pltpu.VMEM),
        scratch_shapes=[pltpu.SMEM(a.shape, a.dtype) for a in ints]
        + [
            pltpu.VMEM(q.shape, bf16),
            pltpu.VMEM(new.shape, bf16),
            pltpu.VMEM((kv_local, 2, slots, block_len, width), bf16),
            pltpu.VMEM((2, keys, width), bf16),
            pltpu.VMEM((n_x, kv_local // 2, 16, width), bf16),
            pltpu.VMEM((kv_local // 2, 2, n_x, n_j, 16, width), bf16),
            pltpu.VMEM((2, 8, rows, width), bf16),
            pltpu.VMEM((keys // chunk, rows, chunk), f32),
            per_row,
            per_row,
            per_row,
            pltpu.VMEM((3, rows, width), f32),
            per_row,
            pltpu.VMEM((8, 128), f32),
            pltpu.VMEM((n_i, 8, 128), f32),
            pltpu.VMEM((kv_local, SAMPLES, 16, width), bf16),
            pltpu.VMEM((kv_local, n_i, 16, width), bf16),
            pltpu.VMEM((SAMPLES, 8, 128), f32),
            pltpu.VMEM((n_i, 8, 128), f32),
            pltpu.VMEM((n_x, (kv_local + 1) * 8, width), f32),
            pltpu.VMEM((n_x, (kv_local + 1) * 8, width), f32),
            dma((len(ints),)),
            dma((2,)),
            dma((kv_local,)),
            dma,
            dma((kv_local // 2, n_x)),
            dma((kv_local // 2, n_x)),
            dma((kv_local // 2, n_x)),
            dma((kv_local // 2, n_x)),
            dma,
            dma,
            dma((kv_local,)),
            dma((kv_local,)),
            dma,
            dma,
            dma,
            dma,
        ],
        compiler_params=pltpu.CompilerParams(
            collective_id=0, has_side_effects=True, vmem_limit_bytes=60 << 20
        ),
        name="decode_attention",
    )(*ints, q, new, suffix, prefix_kv)
    return out.reshape(steps, rows_dev, heads * width)


def solution(mesh):
    return jax.shard_map(
        functools.partial(local, mesh.shape["rows"], mesh.shape["prefix"]),
        mesh=mesh,
        in_specs=(
            P(None, ("rows", "prefix"), None, None),
            P(None, None, ("rows", "prefix"), None, None),
            P(None, ("rows", "prefix"), None, None, None),
            P(("rows", "prefix")),
            P(),
            P(None, "prefix", "rows", None, None),
            P("prefix", None),
            P("prefix", None),
            P("prefix"),
        ),
        out_specs=P(None, ("rows", "prefix"), None),
        check_vma=False,
    )
```

time: 48.4 us -> 45.3 us (0.936)
  Pallas kernels: 45.4 us -> 42.4 us
    pallas_call x1, Pallas kernels: 45.4 us -> 42.4 us  [local(): pl.pallas_call(functools.partial(kernel, n_x, n_i, block_len, slots), out...]
    reshape x1 -> x0, local copies, waits for them, and re-layouts: 1.39 us -> none  [local(): return out.reshape(steps, rows_dev, heads * width)]
    unnamed x0 -> x1, local copies, waits for them, and re-layouts: none -> 1.39 us
where the time goes in v2:
time: 45.3 us; the launch traced here: 45.1 us
  Pallas kernels  42.4 us (94%)
  local copies, waits for them, and re-layouts  1.39 us (3%)
  between operations  1.3 us (3%)
    pallas_call x1, Pallas kernels, local(): pl.pallas_call(functools.partial(kernel, n_x, n_i, block_len, slots), out...  42.4 us
    unnamed x1, local copies, waits for them, and re-layouts  1.39 us

profile of v2, /device:TPU:1, one launch (start us, length us, event | category | flops | bytes accessed | tf_op | source)
XLA Modules:
  0.0 45.1 jit_solution(1985193246589800942)
XLA Ops:
  1.3 42.4 %decode_attention.1 = bf16[4,4096]{1,0:T(4,128)(2,1)} custom-call(s32[1,10]{1,0:T(1,128)} %prompt_hbm.1, s32[1,10]{1,0:T(1,128)} %index_hbm.1, s32[1]{0:T(128)S(6)} %copy.12.count_hbm, s32[8]{0:T(128)} %prefix_len_hbm.1, s32[1]{0:T(128)S(6)} %copy.11.suffix_len_hbm, bf16[128,128]{1,0:T(8,128)(2,1)} %bitcast.6, bf16[2,64,128]{2,1,0:T(8,128)(2,1)} %bitcast.7, ...), custom_call_target="tpu_custom_call" | custom-call | tf_op jit(solution)/shard_map/decode_attention/pallas_call | solution.py:468
  43.7 1.4 %copy.13 = bf16[4,1,4096]{2,0,1:T(4,128)(2,1)} copy(bf16[4,1,4096]{2,0,1:T(4,128)(2,1)} %bitcast.5) | data formatting | bytes 65536

commit v3 on v2

--- a/solution.py
+++ b/solution.py
@@ -62,8 +62,12 @@
     part_in,
     stat,
     stat_in,
+    last_stat,
+    last_stat_in,
     fin,
     fin_in,
+    last_fin,
+    last_fin_in,
     int_sem,
     small_sem,
     kv_sem,
@@ -78,8 +82,12 @@
     part_recv,
     stat_send,
     stat_recv,
+    last_stat_send,
+    last_stat_recv,
     fin_send,
     fin_recv,
+    last_fin_send,
+    last_fin_recv,
 ):
     me_x = lax.axis_index("rows")
     me_i = lax.axis_index("prefix")
@@ -95,10 +103,14 @@
     pairs = kv_local // 2
 
     def peer(d):
-        return lax.rem(me_i + d, n_i)
-
-    def sample(i):
-        return lax.rem(i, 2) * half_j + lax.rem(i, SAMPLES) // 2
+        to = me_i + d
+        return jnp.where(to >= n_i, to - n_i, to)
+
+    me_sample = lax.rem(me_i, SAMPLES)
+
+    def sample(d):
+        n = me_sample + d % SAMPLES
+        return jnp.where(n >= SAMPLES, n - SAMPLES, n)
 
     def on_core(d):
         return lax.rem(me_j + d, n_j) * 2 + me_c
@@ -281,24 +293,31 @@
             push(mine, mine, forward_send.at[pair, dx], forward_recv.at[pair, dx], sibling)
 
     def push_part(k):
-        def one(d, carry):
-            to = peer(d)
+        for d in range(1, n_i):
             push(
-                part.at[k, sample(to)],
+                part.at[k, sample(d)],
                 part_in.at[k, me_i],
                 part_send.at[k],
                 part_recv.at[k],
-                (me_x, to),
+                (me_x, peer(d)),
             )
-            return carry
-
-        lax.fori_loop(1, n_i, one, 0)
-        part_in[k, me_i] = part[k, sample(me_i)]
-
-    def push_stat(d, carry):
-        to = peer(d)
-        push(stat.at[sample(to)], stat_in.at[me_i], stat_send, stat_recv, (me_x, to))
-        return carry
+        part_in[k, me_i] = part[k, me_sample]
+
+    def push_stats(last):
+        here, there = (last_stat, last_stat_in) if last else (stat, stat_in)
+        send, recv = (last_stat_send, last_stat_recv) if last else (stat_send, stat_recv)
+        turned = packed[...].T
+        first = pltpu.roll(turned[:8], base, 1)
+        second = pltpu.roll(turned[8:16], base + 8, 1)
+        for n in range(SAMPLES):
+            shift = (128 - 8 * n) % 128
+            one, two = (pltpu.roll(a, shift, 1) if shift else a for a in (first, second))
+            both = jnp.where(in_first, one, jnp.where(in_second, two, 0.0))
+            here[n] = both[6:8] if last else both
+
+        for d in range(1, n_i):
+            push(here.at[sample(d)], there.at[me_i], send, recv, (me_x, peer(d)))
+        there[me_i] = here[me_sample]
 
     forward_q(0)
     for k in range(kv_local):
@@ -311,7 +330,7 @@
             for half in range(2):
                 for x in range(n_x):
                     v = q_all[pair, :, x, pl.ds(half * half_j, half_j)].astype(f32)
-                    v = v.reshape(SAMPLES, 2, 8, 128)
+                    v = v.swapaxes(0, 1).reshape(SAMPLES, 2, 8, 128)
                     for n in range(2):
                         q_prompt[n, 2 * x + half] = v[:, n].reshape(rows, 128).astype(bf16)
         elif pair + 1 < pairs:
@@ -357,16 +376,8 @@
         parts = [t.reshape(SAMPLES, 8, 128) for t in (total_a, total_b)]
         part[k] = jnp.concatenate(parts, axis=1).astype(bf16)
         push_part(k)
-
-    turned = packed[...].T
-    first = pltpu.roll(turned[:8], base, 1)
-    second = pltpu.roll(turned[8:16], base + 8, 1)
-    for n in range(SAMPLES):
-        shift = (128 - 8 * n) % 128
-        one, two = (pltpu.roll(a, shift, 1) if shift else a for a in (first, second))
-        stat[n] = jnp.where(in_first, one, jnp.where(in_second, two, 0.0))
-    lax.fori_loop(1, n_i, push_stat, 0)
-    stat_in[me_i] = stat[sample(me_i)]
+        if k >= kv_local - 2:
+            push_stats(k == kv_local - 1)
 
     tag_wait = waiter(tag_in.at[pl.ds(0, n_i - 1)], tag_send, tag_recv)
     tag_wait.wait_recv()
@@ -375,6 +386,9 @@
         for k in range(kv_local)
     ]
     stat_wait = waiter(stat_in.at[pl.ds(0, n_i - 1)], stat_send, stat_recv)
+    last_stat_wait = waiter(
+        last_stat_in.at[pl.ds(0, n_i - 1)], last_stat_send, last_stat_recv
+    )
 
     def side_by_side(ref):
         groups = [functools.reduce(jnp.add, [ref[g * 8 + n] for n in range(8)]) for g in range(n_i // 8)]
@@ -384,47 +398,68 @@
     row = iota((n_x * 8, 1), 0)
     prompt = (row // 8 * 2 + lax.rem(me_i // SAMPLES, 2)).astype(f32)
     same = (lax.rem(key, 8) == lax.rem(row, 8)) & (side_by_side(tag_in)[:1] == prompt)
-    stat_wait.wait_recv()
-    st = side_by_side(stat_in)
-    tile = jnp.zeros((n_x * 8, 128), f32)
-    for k in range(kv_local):
+
+    def combine(k, st):
         part_waits[k].wait_recv()
-        peaks = jnp.where(same, st[k * 2 : k * 2 + 1], masked_score)
+        peaks = jnp.where(same, st[:1], masked_score)
         peak = jnp.max(peaks, axis=1, keepdims=True)
         factor = jnp.where(same, jnp.exp2((peaks - peak) * exponent), 0.0)
-        mass = jnp.sum(factor * st[k * 2 + 1 : k * 2 + 2], axis=1, keepdims=True)
+        mass = jnp.sum(factor * st[1:], axis=1, keepdims=True)
         high = factor.astype(bf16)
         low = (factor - high.astype(f32)).astype(bf16)
         parts = part_in[k].reshape(n_i * 16, 128)
         total = lax.dot_general(high, parts, NN, preferred_element_type=f32)
         total = total + lax.dot_general(low, parts, NN, preferred_element_type=f32)
-        fin[:, k * 8 : k * 8 + 8] = total.reshape(n_x, 8, 128)
+        return total.reshape(n_x, 8, 128), peak, mass
+
+    def push_fin(here, there, send, recv):
+        for d in range(1, n_x):
+            x = mate(d)
+            push(here.at[x], there.at[me_x], send, recv, (x, me_i))
+        there[me_x] = here[me_x]
+        return waiter(there.at[pl.ds(0, n_x - 1)], send, recv)
+
+    def finish(g, k, total, st, at):
+        span = pl.ds((g * kv_local + k) * 8, 8)
+        prefix_peak = st[:, at : at + 1]
+        prefix_mass = st[:, at + 1 : at + 2]
+        peak = own_m[span, :]
+        top = jnp.maximum(prefix_peak, peak)
+        from_prefix = jnp.exp2((prefix_peak - top) * exponent)
+        from_own = jnp.exp2((peak - top) * exponent)
+        numer = from_prefix * total + from_own * own_acc[span, :]
+        denom = from_prefix * prefix_mass + from_own * own_l[span, :]
+        result = (numer / denom).astype(bf16)
+        for n in range(2):
+            head = (g * kv_local + k) * 2 + n
+            out_ref[:, head * 128 : head * 128 + 128] = result[n * 4 : n * 4 + 4]
+
+    early = kv_local - 1
+    stat_wait.wait_recv()
+    st = side_by_side(stat_in)
+    tile = jnp.zeros((n_x * 8, 128), f32)
+    for k in range(early):
+        total, peak, mass = combine(k, st[k * 2 : k * 2 + 2])
+        fin[:, k * 8 : k * 8 + 8] = total
         tile = jnp.where(lane == k * 2, peak, jnp.where(lane == k * 2 + 1, mass, tile))
-    fin[:, kv_local * 8 : kv_local * 8 + 8] = tile.reshape(n_x, 8, 128)
-    for d in range(1, n_x):
-        x = mate(d)
-        push(fin.at[x], fin_in.at[me_x], fin_send, fin_recv, (x, me_i))
-    fin_in[me_x] = fin[me_x]
-    fin_wait = waiter(fin_in.at[pl.ds(0, n_x - 1)], fin_send, fin_recv)
+    fin[:, early * 8 : early * 8 + 8] = tile.reshape(n_x, 8, 128)
+    fin_wait = push_fin(fin, fin_in, fin_send, fin_recv)
+
+    last_stat_wait.wait_recv()
+    total, peak, mass = combine(early, side_by_side(last_stat_in))
+    last_fin[:, :8] = total
+    tile = jnp.where(lane == 0, peak, jnp.where(lane == 1, mass, 0.0))
+    last_fin[:, 8:16] = tile.reshape(n_x, 8, 128)
+    last_fin_wait = push_fin(last_fin, last_fin_in, last_fin_send, last_fin_recv)
+
     fin_wait.wait_recv()
-
     for g in range(n_x):
-        st = fin_in[g, kv_local * 8 : kv_local * 8 + 8]
-        for k in range(kv_local):
-            at = (g * kv_local + k) * 8
-            span = slice(at, at + 8)
-            prefix_peak = st[:, k * 2 : k * 2 + 1]
-            prefix_mass = st[:, k * 2 + 1 : k * 2 + 2]
-            peak = own_m[span, :]
-            top = jnp.maximum(prefix_peak, peak)
-            from_prefix = jnp.exp2((prefix_peak - top) * exponent)
-            from_own = jnp.exp2((peak - top) * exponent)
-            numer = from_prefix * fin_in[g, k * 8 : k * 8 + 8] + from_own * own_acc[span, :]
-            denom = from_prefix * prefix_mass + from_own * own_l[span, :]
-            result = (numer / denom).astype(bf16)
-            for n in range(2):
-                head = (g * kv_local + k) * 2 + n
-                out_ref[:, head * 128 : head * 128 + 128] = result[n * 4 : n * 4 + 4]
+        st = fin_in[g, early * 8 : early * 8 + 8]
+        for k in range(early):
+            finish(g, k, fin_in[g, k * 8 : k * 8 + 8], st, k * 2)
+    last_fin_wait.wait_recv()
+    for g in range(n_x):
+        finish(g, early, last_fin_in[g, :8], last_fin_in[g, 8:16], 0)
 
     for pair in range(pairs):
         for dx in range(n_x):
@@ -436,7 +471,9 @@
         part_waits[k].wait_send()
     tag_wait.wait_send()
     stat_wait.wait_send()
+    last_stat_wait.wait_send()
     fin_wait.wait_send()
+    last_fin_wait.wait_send()
 
 
 def local(
@@ -491,8 +528,12 @@
             pltpu.VMEM((kv_local, n_i, 16, width), bf16),
             pltpu.VMEM((SAMPLES, 8, 128), f32),
             pltpu.VMEM((n_i, 8, 128), f32),
-            pltpu.VMEM((n_x, (kv_local + 1) * 8, width), f32),
-            pltpu.VMEM((n_x, (kv_local + 1) * 8, width), f32),
+            pltpu.VMEM((SAMPLES, 2, 128), f32),
+            pltpu.VMEM((n_i, 2, 128), f32),
+            pltpu.VMEM((n_x, kv_local * 8, width), f32),
+            pltpu.VMEM((n_x, kv_local * 8, width), f32),
+            pltpu.VMEM((n_x, 16, width), f32),
+            pltpu.VMEM((n_x, 16, width), f32),
             dma((len(ints),)),
             dma((2,)),
             dma((kv_local,)),
@@ -505,6 +546,10 @@
             dma,
             dma((kv_local,)),
             dma((kv_local,)),
+            dma,
+            dma,
+            dma,
+            dma,
             dma,
             dma,
             dma,

time: 45.3 us -> 42.5 us (0.938)
  Pallas kernels: 42.4 us -> 39.6 us
    pallas_call x1, Pallas kernels: 42.4 us -> 39.6 us  [local(): pl.pallas_call(functools.partial(kernel, n_x, n_i, block_len, slots), out...]
where the time goes in v3:
time: 42.5 us; the launch traced here: 42.3 us
  Pallas kernels  39.6 us (93%)
  local copies, waits for them, and re-layouts  1.39 us (3%)
  between operations  1.3 us (3%)
    pallas_call x1, Pallas kernels, local(): pl.pallas_call(functools.partial(kernel, n_x, n_i, block_len, slots), out...  39.6 us
    unnamed x1, local copies, waits for them, and re-layouts  1.39 us

profile of v3, /device:TPU:1, one launch (start us, length us, event | category | flops | bytes accessed | tf_op | source)
XLA Modules:
  0.0 42.3 jit_solution(4460084428212389077)
XLA Ops:
  1.3 39.6 %decode_attention.1 = bf16[4,4096]{1,0:T(4,128)(2,1)} custom-call(s32[1,10]{1,0:T(1,128)} %prompt_hbm.1, s32[1,10]{1,0:T(1,128)} %index_hbm.1, s32[1]{0:T(128)S(6)} %copy.12.count_hbm, s32[8]{0:T(128)} %prefix_len_hbm.1, s32[1]{0:T(128)S(6)} %copy.11.suffix_len_hbm, bf16[128,128]{1,0:T(8,128)(2,1)} %bitcast.6, bf16[2,64,128]{2,1,0:T(8,128)(2,1)} %bitcast.7, ...), custom_call_target="tpu_custom_call" | custom-call | tf_op jit(solution)/shard_map/decode_attention/pallas_call | solution.py:505
  40.9 1.4 %copy.13 = bf16[4,1,4096]{2,0,1:T(4,128)(2,1)} copy(bf16[4,1,4096]{2,0,1:T(4,128)(2,1)} %bitcast.5) | data formatting | bytes 65536

commit v4 on v3

--- a/solution.py
+++ b/solution.py
@@ -113,29 +113,24 @@
         return jnp.where(n >= SAMPLES, n - SAMPLES, n)
 
     def on_core(d):
-        return lax.rem(me_j + d, n_j) * 2 + me_c
+        to = me_i + 2 * d
+        return jnp.where(to >= n_i, to - n_i, to)
 
     def mate(d):
-        return lax.rem(me_x + d, n_x)
+        to = me_x + d
+        return jnp.where(to >= n_x, to - n_x, to)
 
     barrier = pltpu.get_barrier_semaphore()
-
-    def greet_other(j, carry):
+    for j in range(n_j):
         pl.semaphore_signal(
             barrier, inc=1, device_id=(me_x, j * 2 + other_c), device_id_type=MESH
         )
-        return carry
-
-    lax.fori_loop(0, n_j, greet_other, 0)
     for dx in range(n_x):
 
-        def greet(d, carry, dx=dx):
+        for d in range(1 if dx == 0 else 0, n_j):
             pl.semaphore_signal(
                 barrier, inc=1, device_id=(mate(dx), on_core(d)), device_id_type=MESH
             )
-            return carry
-
-        lax.fori_loop(1 if dx == 0 else 0, n_j, greet, 0)
 
     small_copies = [
         pltpu.make_async_copy(q_hbm, q_ref, small_sem.at[0]),
@@ -194,11 +189,10 @@
             device_id_type=MESH,
         ).start()
 
-    for pair in range(pairs):
+    def push_pair(pair):
         for dx in X_ORDER:
-
-            def push_q(d, carry, pair=pair, dx=dx):
-                x = mate(dx)
+            x = mate(dx)
+            for d in range(1 if dx == 0 else 0, n_j):
                 push(
                     q_own.at[x, pair],
                     q_all.at[pair, me_c, me_x, me_j],
@@ -206,9 +200,8 @@
                     q_recv.at[pair, dx],
                     (x, on_core(d)),
                 )
-                return carry
-
-            lax.fori_loop(1 if dx == 0 else 0, n_j, push_q, 0)
+
+    push_pair(0)
     for copy in kv_copies:
         copy.start()
 
@@ -230,11 +223,6 @@
     tag[...] = jnp.broadcast_to(tags, (8, 128))
     tag_in[me_i] = tag[...]
 
-    def push_tag(d, carry):
-        push(tag, tag_in.at[me_i], tag_send, tag_recv, (me_x, peer(d)))
-        return carry
-
-    lax.fori_loop(1, n_i, push_tag, 0)
     chunk = own_s.shape[2]
     chunks = own_s.shape[0]
     suffix_len = suffix_len_ref[0]
@@ -276,6 +264,8 @@
     own_l[...] = mass
     own_m[...] = jnp.broadcast_to(own_peak, (rows, 128))
 
+    push_pair(1)
+
     column = iota((1, block_len), 1)
     ones = jnp.ones((block_len, 128), bf16)
     in_a = [jnp.where(prompt_ref[0, j] == prompt_a, 1, 0) for j in range(slots)]
@@ -320,6 +310,8 @@
         there[me_i] = here[me_sample]
 
     forward_q(0)
+    for d in range(1, n_i):
+        push(tag, tag_in.at[me_i], tag_send, tag_recv, (me_x, peer(d)))
     for k in range(kv_local):
         pair = k // 2
         if k % 2 == 0:

time: 42.5 us -> 41.7 us (0.981)
  Pallas kernels: 39.6 us -> 38.8 us
    pallas_call x1, Pallas kernels: 39.6 us -> 38.8 us  [local(): pl.pallas_call(functools.partial(kernel, n_x, n_i, block_len, slots), out...]
where the time goes in v4:
time: 41.7 us; the launch traced here: 41.5 us
  Pallas kernels  38.8 us (93%)
  local copies, waits for them, and re-layouts  1.39 us (3%)
  between operations  1.3 us (3%)
    pallas_call x1, Pallas kernels, local(): pl.pallas_call(functools.partial(kernel, n_x, n_i, block_len, slots), out...  38.8 us
    unnamed x1, local copies, waits for them, and re-layouts  1.39 us

profile of v4, /device:TPU:1, one launch (start us, length us, event | category | flops | bytes accessed | tf_op | source)
XLA Modules:
  0.0 41.5 jit_solution(10101018629616377231)
XLA Ops:
  1.3 38.8 %decode_attention.1 = bf16[4,4096]{1,0:T(4,128)(2,1)} custom-call(s32[1,10]{1,0:T(1,128)} %prompt_hbm.1, s32[1,10]{1,0:T(1,128)} %index_hbm.1, s32[1]{0:T(128)S(6)} %copy.12.count_hbm, s32[8]{0:T(128)} %prefix_len_hbm.1, s32[1]{0:T(128)S(6)} %copy.11.suffix_len_hbm, bf16[128,128]{1,0:T(8,128)(2,1)} %bitcast.6, bf16[2,64,128]{2,1,0:T(8,128)(2,1)} %bitcast.7, ...), custom_call_target="tpu_custom_call" | custom-call | tf_op jit(solution)/shard_map/decode_attention/pallas_call | solution.py:497
  40.1 1.4 %copy.13 = bf16[4,1,4096]{2,0,1:T(4,128)(2,1)} copy(bf16[4,1,4096]{2,0,1:T(4,128)(2,1)} %bitcast.5) | data formatting | bytes 65536

commit v5 on v4

--- a/solution.py
+++ b/solution.py
@@ -17,6 +17,16 @@
 NT = (((1,), (1,)), ((), ()))
 NN = (((1,), (0,)), ((), ()))
 X_ORDER = (0, 1, 3, 2)
+
+
+def far_first(n_i):
+    n = n_i // 8
+
+    def hops(d):
+        z, y = d // 8, d % 8 // 2
+        return min(z, n - z) + min(y, 4 - y)
+
+    return sorted(range(1, n_i), key=hops, reverse=True)
 
 
 def iota(shape, dim):
@@ -283,7 +293,7 @@
             push(mine, mine, forward_send.at[pair, dx], forward_recv.at[pair, dx], sibling)
 
     def push_part(k):
-        for d in range(1, n_i):
+        for d in far_first(n_i):
             push(
                 part.at[k, sample(d)],
                 part_in.at[k, me_i],
@@ -305,13 +315,15 @@
             both = jnp.where(in_first, one, jnp.where(in_second, two, 0.0))
             here[n] = both[6:8] if last else both
 
-        for d in range(1, n_i):
+        for d in far_first(n_i):
             push(here.at[sample(d)], there.at[me_i], send, recv, (me_x, peer(d)))
         there[me_i] = here[me_sample]
 
     forward_q(0)
     for d in range(1, n_i):
         push(tag, tag_in.at[me_i], tag_send, tag_recv, (me_x, peer(d)))
+    for copy in kv_copies:
+        copy.wait()
     for k in range(kv_local):
         pair = k // 2
         if k % 2 == 0:
@@ -325,9 +337,6 @@
                     v = v.swapaxes(0, 1).reshape(SAMPLES, 2, 8, 128)
                     for n in range(2):
                         q_prompt[n, 2 * x + half] = v[:, n].reshape(rows, 128).astype(bf16)
-        elif pair + 1 < pairs:
-            forward_q(pair + 1)
-        kv_copies[k].wait()
 
         accs, ms = [], []
         peaks = jnp.full((rows, 128), masked_score, f32)
@@ -367,6 +376,8 @@
             total_b = total_b + jnp.where(in_a[j] == 1, 0.0, taken)
         parts = [t.reshape(SAMPLES, 8, 128) for t in (total_a, total_b)]
         part[k] = jnp.concatenate(parts, axis=1).astype(bf16)
+        if k == 0:
+            forward_q(1)
         push_part(k)
         if k >= kv_local - 2:
             push_stats(k == kv_local - 1)

time: 41.7 us -> 41.7 us (level)
  no operation moved by 1% of the time
where the time goes in v5:
time: 41.7 us; the launch traced here: 41.5 us
  Pallas kernels  38.9 us (93%)
  local copies, waits for them, and re-layouts  1.39 us (3%)
  between operations  1.3 us (3%)
    pallas_call x1, Pallas kernels, local(): pl.pallas_call(functools.partial(kernel, n_x, n_i, block_len, slots), out...  38.9 us
    unnamed x1, local copies, waits for them, and re-layouts  1.39 us

profile of v5, /device:TPU:1, one launch (start us, length us, event | category | flops | bytes accessed | tf_op | source)
XLA Modules:
  0.0 41.5 jit_solution(8039614549213237743)
XLA Ops:
  1.3 38.9 %decode_attention.1 = bf16[4,4096]{1,0:T(4,128)(2,1)} custom-call(s32[1,10]{1,0:T(1,128)} %prompt_hbm.1, s32[1,10]{1,0:T(1,128)} %index_hbm.1, s32[1]{0:T(128)S(6)} %copy.12.count_hbm, s32[8]{0:T(128)} %prefix_len_hbm.1, s32[1]{0:T(128)S(6)} %copy.11.suffix_len_hbm, bf16[128,128]{1,0:T(8,128)(2,1)} %bitcast.6, bf16[2,64,128]{2,1,0:T(8,128)(2,1)} %bitcast.7, ...), custom_call_target="tpu_custom_call" | custom-call | tf_op jit(solution)/shard_map/decode_attention/pallas_call | solution.py:508
  40.2 1.4 %copy.13 = bf16[4,1,4096]{2,0,1:T(4,128)(2,1)} copy(bf16[4,1,4096]{2,0,1:T(4,128)(2,1)} %bitcast.5) | data formatting | bytes 65536
